TPU v7x, 32 devices: a whole 2x2x4 slice. The times are simulated.
32 devices in a mesh: grp: 2 (over y), exp: 4 (over z), wsh: 4 (over x, core).
Axes of the slice: x: 2, y: 2, z: 4, core: 2. Of those that a mesh axis runs over, the one named last changes fastest.
Arguments:
- hidden_in: bfloat16 [4096, 2880], P(('grp', 'exp', 'wsh')), parts along dimension 0
- norm_gain: float32 [2880], replicated, may hold values from 0.1 to 1.9
- expert_ids: int32 [4096, 4], P(('grp', 'exp', 'wsh')), parts along dimension 0, may hold values from 0 to 3, as said below
- gate_weights: bfloat16 [4096, 4], P(('grp', 'exp', 'wsh')), parts along dimension 0, may hold values from 0.049804688 to 1
- gate_up_codes: bfloat16 [4, 2880, 2880], P('exp', None, 'wsh'), may hold values from -6 to 6
- gate_up_scales: int32 [4, 90, 2880], P('exp', None, 'wsh'), may hold values from 7 to 9
- down_codes: bfloat16 [4, 1440, 2880], P('exp', None, 'wsh'), may hold values from -6 to 6
- down_scales: int32 [4, 45, 2880], P('exp', None, 'wsh'), may hold values from 6 to 8
Outputs:
- mixture: bfloat16 [4096, 2880], P(('grp', 'exp', 'wsh')), parts along dimension 0
There are 2 independent parts, one for each index of `grp`. A program takes and returns all parts, laid end to end along the dimension named above; an argument that names none is the same for every part. Nothing has to cross between parts.
Inputs may be any that keep to these rules, and one draw needn't show every extreme that they name: `expert_ids`: each row names 4 different experts; one expert, drawn anew in each draw, is named by every token, so it fills all 64 rows from every block.
All inputs are finite; a program needn't handle non-finite values.
Results may differ from a plain program's by a relative error of at most 0.0067.
Values may be sent and summed in bfloat16 or wider, within the bound.
A program may use at most 128 MiB of HBM per device.

v0:
```python
import jax
import jax.numpy as jnp
from jax import lax
from jax.sharding import PartitionSpec as P

EPSILON = 1e-05
SWISH_ALPHA = 1.702


def normalize(hidden_in, norm_gain):
    values = hidden_in.astype(jnp.float32)
    meansq = jnp.mean(values * values, axis=-1, keepdims=True)
    return (values * lax.rsqrt(meansq + EPSILON) * norm_gain).astype(jnp.bfloat16)


def expand_block(mantissa, exponent):
    groups = exponent.shape[-2]
    factor = jnp.exp2(-exponent.astype(jnp.float32)).astype(jnp.bfloat16)
    shaped = mantissa.reshape(
        mantissa.shape[:-2] + (groups, mantissa.shape[-2] // groups, mantissa.shape[-1])
    )
    return (shaped * factor[..., :, None, :]).reshape(mantissa.shape)


def activate(gate_up, inner_width):
    gate_part = gate_up[:, :inner_width]
    upward = gate_up[:, inner_width:]
    return ((upward + 1.0) * gate_part * jax.nn.sigmoid(SWISH_ALPHA * gate_part)).astype(
        jnp.bfloat16
    )


def block_slots(block_ids, expert_count, capacity):
    rows, picks = block_ids.shape
    labels = jnp.arange(expert_count, dtype=jnp.int32)
    onehot = (block_ids.reshape(rows * picks)[:, None] == labels[None, :]).astype(jnp.int32)
    earlier = jnp.cumsum(onehot, axis=0) - onehot
    ranking = jnp.sum(earlier * onehot, axis=1).reshape(rows, picks)
    return jnp.where(ranking < capacity, ranking, -1)


def per_device(
    hidden_in,
    norm_gain,
    expert_ids,
    gate_weights,
    gate_up_codes,
    gate_up_scales,
    down_codes,
    down_scales,
):
    normed = normalize(hidden_in, norm_gain)
    tok_rows, model_width = hidden_in.shape
    picks_per = expert_ids.shape[1]
    owners = lax.axis_size("exp")
    capacity = min(tok_rows // 2, tok_rows * picks_per // owners)
    slot_index = block_slots(expert_ids, owners, capacity)
    target = jnp.where(slot_index >= 0, expert_ids * capacity + slot_index, -1)
    positions = jnp.arange(owners * capacity, dtype=jnp.int32)
    matches = target[:, :, None] == positions[None, None, :]
    placing = jnp.any(matches, axis=1).astype(jnp.bfloat16)
    outgoing = jnp.einsum("ts,td->sd", placing, normed, preferred_element_type=jnp.float32).astype(
        jnp.bfloat16
    )
    outgoing = outgoing.reshape(owners, capacity, model_width)
    inner_width = down_codes.shape[1]
    arrived = lax.all_to_all(outgoing, "exp", split_axis=0, concat_axis=0, tiled=True)
    arrived = arrived.reshape(owners * capacity, model_width)
    shard_piece = lax.all_gather((gate_up_codes[0], gate_up_scales[0]), "wsh", axis=1, tiled=True)
    gate_up = jnp.dot(
        arrived, expand_block(shard_piece[0], shard_piece[1]), preferred_element_type=jnp.float32
    )
    hidden_act = activate(gate_up, inner_width)
    shard_piece = lax.all_gather((down_codes[0], down_scales[0]), "wsh", axis=1, tiled=True)
    expert_out = jnp.dot(
        hidden_act, expand_block(shard_piece[0], shard_piece[1]), preferred_element_type=jnp.float32
    )
    expert_rows = expert_out.astype(jnp.bfloat16).reshape(owners, capacity, model_width)
    came_back = lax.all_to_all(expert_rows, "exp", split_axis=0, concat_axis=0, tiled=True).reshape(
        owners * capacity, model_width
    )
    weighting = jnp.sum(
        jnp.where(matches, gate_weights[:, :, None], jnp.zeros((), jnp.bfloat16)), axis=1
    )
    mixture = jnp.dot(weighting, came_back, preferred_element_type=jnp.float32)
    return mixture.astype(jnp.bfloat16)


def solution(mesh):
    placed = (
        P(("grp", "exp", "wsh"), None),
        P(),
        P(("grp", "exp", "wsh"), None),
        P(("grp", "exp", "wsh"), None),
        P("exp", None, "wsh"),
        P("exp", None, "wsh"),
        P("exp", None, "wsh"),
        P("exp", None, "wsh"),
    )
    return jax.shard_map(
        per_device,
        mesh=mesh,
        in_specs=placed,
        out_specs=P(("grp", "exp", "wsh"), None),
        check_vma=False,
    )
```

profile of v0, /device:TPU:0, one launch (start us, length us, event | category | flops | bytes accessed | tf_op | source)
XLA Modules:
  0.0 372.9 jit_solution(6530417374998840021)
XLA Ops:
  6.5 12.0 %copy.55 = bf16[1,1440,720]{1,0,2:T(2,128)(2,1)} copy(bf16[1,1440,720]{2,1,0:T(8,128)(2,1)} %param.14) | data formatting | bytes 4147200 | tf_op args[6]
  18.7 0.7 all-gather.7.cloned.1.call-update
  19.4 0.1 copy.46
  19.7 0.1 copy.49
  19.9 1.2 reduce-window.6
  21.1 0.2 slice_reduce_fusion
  21.3 0.2 reduce-window.9
  21.8 0.2 fusion.13
  22.0 0.4 fusion
  22.4 0.6 convolution_convert_fusion
  23.0 1.7 copy.51
  24.7 6.5 %all-to-all-start = ((bf16[4,64,2880]{2,1,0:T(8,128)(2,1)}), bf16[4,64,2880]{2,1,0:T(8,128)(2,1)}, u32[]{:S(2)}, u32[]{:S(2)}) async-start(bf16[4,64,2880]{2,1,0:T(8,128)(2,1)} %bitcast.1), calls=%async_computation | async-start | bytes 3014656 | tf_op jit(solution)/shard_map/all_to_all | solution.py:67
  31.2 0.9 copy.53
  32.1 0.9 copy.57
  32.9 19.4 %all-gather.3 = s32[1,45,2880]{1,0,2:T(1,128)S(1)} all-gather(s32[1,45,720]{1,0,2:T(1,128)S(1)} %copy.57), channel_id=5, replica_groups=mesh['grp'=2,'exp'=4,'wsh'=4] {'wsh'}, dimensions={2}, use_global_device_ids=true | all-gather | bytes 648000 | tf_op jit(solution)/shard_map/all_gather | solution.py:74
  52.3 1.7 copy.58
  54.0 20.7 %all-gather.1 = s32[1,90,2880]{1,0,2:T(1,128)S(1)} all-gather(s32[1,90,720]{1,0,2:T(1,128)S(1)} %copy.53), channel_id=3, replica_groups=mesh['grp'=2,'exp'=4,'wsh'=4] {'wsh'}, dimensions={2}, use_global_device_ids=true | all-gather | bytes 1296000 | tf_op jit(solution)/shard_map/all_gather | solution.py:69
  74.8 1.8 copy.54
  76.7 0.2 fusion.12
  76.9 72.4 %all-gather.9.cloned.1.call-done = bf16[1,1440,2880]{1,0,2:T(2,128)(2,1)} async-done(((bf16[1,1440,720]{1,0,2:T(2,128)(2,1)}), bf16[1,1440,2880]{1,0,2:T(2,128)(2,1)}) %all-gather.9.cloned.1.call-update) | async-done | bytes 8294416 | tf_op jit(solution)/shard_map/all_gather | solution.py:74
  149.2 38.7 %copy.56 = bf16[1,1440,2880]{2,1,0:T(8,128)(2,1)} copy(bf16[1,1440,2880]{1,0,2:T(2,128)(2,1)} %all-gather.9.cloned.1.call-done) | data formatting | bytes 16588800 | tf_op jit(solution)/shard_map/all_gather | solution.py:74
  187.9 7.7 %bitcast_multiply_fusion.1 = bf16[1440,2880]{1,0:T(8,128)(2,1)} fusion(bf16[1,1440,2880]{2,1,0:T(8,128)(2,1)} %copy.56, bf16[45,2880]{1,0:T(8,128)(2,1)S(1)} %fusion.15), kind=kLoop, calls=%fused_computation.1 | loop fusion | flops 4147200 | bytes 16848000 | tf_op jit(solution)/shard_map/mul | solution.py:22
  195.6 65.1 %all-gather.7.cloned.1.call-done = bf16[1,2880,2880]{1,2,0:T(8,128)(2,1)} async-done(((bf16[1,2880,720]{1,2,0:T(8,128)(2,1)}), bf16[1,2880,2880]{1,2,0:T(8,128)(2,1)}) %all-gather.7.cloned.1.call-update) | async-done | bytes 16588816 | tf_op jit(solution)/shard_map/all_gather | solution.py:69
  260.8 23.7 %copy.52 = bf16[1,2880,2880]{2,1,0:T(8,128)(2,1)} copy(bf16[1,2880,2880]{1,2,0:T(8,128)(2,1)} %all-gather.7.cloned.1.call-done) | data formatting | bytes 33177600 | tf_op jit(solution)/shard_map/all_gather | solution.py:69
  284.4 14.6 %bitcast_multiply_fusion = bf16[2880,2880]{1,0:T(8,128)(2,1)} fusion(bf16[1,2880,2880]{2,1,0:T(8,128)(2,1)} %copy.52, bf16[90,2880]{1,0:T(8,128)(2,1)S(1)} %fusion.12), kind=kLoop, calls=%fused_computation | loop fusion | flops 8294400 | bytes 33696000 | tf_op jit(solution)/shard_map/mul | solution.py:22
  299.0 14.9 %fusion.23 = f32[256,2880]{0,1:T(8,128)} fusion(bf16[256,2880]{1,0:T(8,128)(2,1)} %bitcast.2, bf16[2880,2880]{1,0:T(8,128)(2,1)} %bitcast_multiply_fusion), kind=kOutput, calls=%fused_computation.41 | convolution fusion | flops 4246732800 | bytes 21012480 | tf_op jit(solution)/shard_map/dot_general | solution.py:70
  313.9 8.1 %convolution_convert_fusion.1 = bf16[256,2880]{0,1:T(8,128)(2,1)S(1)} fusion(bf16[1440,2880]{1,0:T(8,128)(2,1)} %bitcast_multiply_fusion.1, f32[256,2880]{0,1:T(8,128)} %fusion.23), kind=kOutput, calls=%fused_computation.3 | convolution fusion | flops 2127052800 | bytes 12718080 | tf_op jit(solution)/shard_map/dot_general | solution.py:75
  322.0 1.7 copy.59
  323.8 4.7 %all-to-all-start.1 = ((bf16[4,64,2880]{2,1,0:T(8,128)(2,1)}), bf16[4,64,2880]{2,1,0:T(8,128)(2,1)S(1)}, u32[]{:S(2)}, u32[]{:S(2)}) async-start(bf16[4,64,2880]{2,1,0:T(8,128)(2,1)} %bitcast.9), calls=%async_computation.1 | async-start | bytes 3014656 | tf_op jit(solution)/shard_map/all_to_all | solution.py:79
  328.5 0.2 fusion.16
  328.7 35.8 %all-to-all-done.1 = bf16[4,64,2880]{2,1,0:T(8,128)(2,1)S(1)} async-done(((bf16[4,64,2880]{2,1,0:T(8,128)(2,1)}), bf16[4,64,2880]{2,1,0:T(8,128)(2,1)S(1)}, u32[]{:S(2)}, u32[]{:S(2)}) %all-to-all-start.1) | async-done | bytes 1474592 | tf_op jit(solution)/shard_map/all_to_all | solution.py:79
  364.5 1.6 convolution_convert_fusion.2
  (27 shorter events, 0.7 us)
Async XLA Ops:
  6.5 142.7 %all-gather.9.cloned.1.call-start = ((), (), s32[]{:S(2)}) async-start(), calls=%async_computation.3 | async-start | bytes 22118400 | tf_op jit(solution)/shard_map/all_gather | solution.py:74
  18.6 0.8 copy-start.4
  18.6 3.4 copy-start
  18.6 3.8 %copy-start.3 = (f32[2880]{0:T(1024)S(1)}, f32[2880]{0:T(1024)}, u32[]{:S(2)}) copy-start(f32[2880]{0:T(1024)} %param.9) | copy-start | bytes 34564
  18.6 242.1 %all-gather.7.cloned.1.call-start = ((), (), s32[]{:S(2)}) async-start(), calls=%async_computation.2 | async-start | bytes 21196800 | tf_op jit(solution)/shard_map/all_gather | solution.py:69
  24.7 6.5 %copy-start.1 = (s32[1,90,720]{2,0,1:T(1,128)S(1)}, s32[1,90,720]{2,0,1:T(1,128)}, u32[]{:S(2)}) copy-start(s32[1,90,720]{2,0,1:T(1,128)} %param.13) | copy-start | bytes 777604
  24.7 7.3 %copy-start.2 = (s32[1,45,720]{2,0,1:T(1,128)S(1)}, s32[1,45,720]{2,0,1:T(1,128)}, u32[]{:S(2)}) copy-start(s32[1,45,720]{2,0,1:T(1,128)} %param.15) | copy-start | bytes 388804
  24.7 274.3 %all-to-all-start = ((bf16[4,64,2880]{2,1,0:T(8,128)(2,1)}), bf16[4,64,2880]{2,1,0:T(8,128)(2,1)}, u32[]{:S(2)}, u32[]{:S(2)}) async-start(bf16[4,64,2880]{2,1,0:T(8,128)(2,1)} %bitcast.1), calls=%async_computation | async-start | bytes 3014656 | tf_op jit(solution)/shard_map/all_to_all | solution.py:67
  323.8 4.7 %copy-start.5 = (bf16[128,4]{0,1:T(4,128)(2,1)S(1)}, bf16[128,4]{0,1:T(4,128)(2,1)}, u32[]{:S(2)}) copy-start(bf16[128,4]{0,1:T(4,128)(2,1)} %param.11) | copy-start | bytes 3076
  323.8 40.7 %all-to-all-start.1 = ((bf16[4,64,2880]{2,1,0:T(8,128)(2,1)}), bf16[4,64,2880]{2,1,0:T(8,128)(2,1)S(1)}, u32[]{:S(2)}, u32[]{:S(2)}) async-start(bf16[4,64,2880]{2,1,0:T(8,128)(2,1)} %bitcast.9), calls=%async_computation.1 | async-start | bytes 3014656 | tf_op jit(solution)/shard_map/all_to_all | solution.py:79
Sparse Core Ops, SparseCore 0:
  18.7 130.4 all-gather.8
  150.8 109.9 all-gather.6
where the time goes:
time: 375 us; the launch traced here: 373 us
  waiting for transfers between devices  174 us (46%)
  local copies, waits for them, and re-layouts  83.9 us (22%)
  blocking collectives  40.2 us (11%)
  matrix products  25.2 us (7%)
  other arithmetic  24.9 us (7%)
  between operations  13.6 us (4%)
  starting transfers between devices  11.2 us (3%)
    all_gather x1, waiting for transfers between devices, per_device(): lax.all_gather((down_codes[0], down_scales[0]), 'wsh', axis=1, tiled=True)  72.4 us
    all_gather x1, waiting for transfers between devices, per_device(): lax.all_gather((gate_up_codes[0], gate_up_scales[0]), 'wsh', axis=1, tile...  65.1 us
    all_gather x2, local copies, waits for them, and re-layouts, per_device(): lax.all_gather((down_codes[0], down_scales[0]), 'wsh', axis=1, tiled=True)  40.4 us
    all_to_all x1, waiting for transfers between devices, per_device(): lax.all_to_all(expert_rows, 'exp', split_axis=0, concat_axis=0, tiled=True)  35.8 us
    all_gather x2, local copies, waits for them, and re-layouts, per_device(): lax.all_gather((gate_up_codes[0], gate_up_scales[0]), 'wsh', axis=1, tile...  25.5 us
    mul x2, other arithmetic, expand_block(): return (shaped * factor[..., :, None, :]).reshape(mantissa.shape)  22.4 us
    all_gather x1, blocking collectives, per_device(): lax.all_gather((gate_up_codes[0], gate_up_scales[0]), 'wsh', axis=1, tile...  20.7 us
    all_gather x1, blocking collectives, per_device(): lax.all_gather((down_codes[0], down_scales[0]), 'wsh', axis=1, tiled=True)  19.4 us
  transfers between devices with their start and end apart: 4, of which 3 were waited for; matrix products, arithmetic and copies ran while one was open for 26% of the time, Pallas kernels for 0%

commit v1 on v0

--- a/solution.py
+++ b/solution.py
@@ -1,6 +1,8 @@
 import jax
 import jax.numpy as jnp
 from jax import lax
+from jax.experimental import pallas as pl
+from jax.experimental.pallas import tpu as pltpu
 from jax.sharding import PartitionSpec as P
 
 EPSILON = 1e-05
@@ -86,6 +88,354 @@
     return mixture.astype(jnp.bfloat16)
 
 
+MESH = pl.DeviceIdType.MESH
+TILE = 256
+GROUP = 32
+
+
+def fused_kernel(
+    hid, gain, ids, gates, guc, gus, dnc, dns, out,
+    stage_g, stage_d, fac_g, fac_d, wg, wd, nrm, weighting, og, xb, first, act, res, back,
+    load_sem, xs, xr, ys, yr, zs, zr, cs, cr, act_s, act_r, rs, rr,
+):
+    grp = lax.axis_index("grp")
+    z = lax.axis_index("exp")
+    w = lax.axis_index("wsh")
+    x = w // 2
+    c = w % 2
+    slot = z * 2 + c
+    mate = x * 2 + (1 - c)
+    across = (1 - x) * 2 + c
+    depth, width = stage_g.shape
+    inner = stage_d.shape[0]
+    half_g, half_d = depth // 2, inner // 2
+    step_g, step_d = half_g // 3, half_d // 3
+    tokens = hid.shape[0]
+    cap = og.shape[1]
+
+    loads = []
+    for k in range(2):
+        part = (grp + k) % 2
+        rows = pl.ds(pl.multiple_of(part * half_g, 16), half_g)
+        loads.append(pltpu.make_async_copy(guc.at[0, rows], stage_g.at[rows], load_sem.at[k]))
+    loads.append(pltpu.make_async_copy(dnc.at[0], stage_d, load_sem.at[2]))
+    for load in loads:
+        load.start()
+
+    barrier = pltpu.get_barrier_semaphore()
+    pl.semaphore_signal(barrier, inc=1, device_id={"wsh": across}, device_id_type=MESH)
+    pl.semaphore_signal(barrier, inc=1, device_id={"grp": 1 - grp}, device_id_type=MESH)
+    for d in range(1, 8):
+        other = (slot + d) % 8
+        pl.semaphore_signal(
+            barrier, inc=1, device_id={"exp": other // 2, "wsh": x * 2 + other % 2}, device_id_type=MESH
+        )
+
+    fac_g[...] = jnp.exp2(-gus[0].astype(jnp.float32))
+    fac_d[...] = jnp.exp2(-dns[0].astype(jnp.float32))
+    wg[0, 2] = jnp.zeros((depth, TILE), jnp.bfloat16)
+    wd[0, 2] = jnp.zeros((inner, TILE), jnp.bfloat16)
+
+    def expand(stage, fac, dest, j, start, groups):
+        lanes = min(TILE, width - j * TILE)
+
+        @pl.loop(0, groups)
+        def _(g):
+            at = start + g
+            row = pl.multiple_of(at * GROUP, GROUP)
+            scale = fac[pl.ds(at, 1), pl.ds(j * TILE, lanes)]
+            scale = jnp.broadcast_to(scale, (GROUP, lanes)).astype(jnp.bfloat16)
+            dest[0, j, pl.ds(row, GROUP), pl.ds(0, lanes)] = (
+                stage[pl.ds(row, GROUP), pl.ds(j * TILE, lanes)] * scale
+            )
+
+    def place(i):
+        buf = wg if i < 9 else wd
+        j, s = (i % 9) // 3, i % 3
+        return buf, j, s, (half_g if i < 9 else half_d), (step_g if i < 9 else step_d)
+
+    def x_copy(i):
+        buf, j, s, half, step = place(i)
+        rows = pl.ds(pl.multiple_of(grp * half + s * step, 16), step)
+        return pltpu.make_async_remote_copy(
+            src_ref=buf.at[0, j, rows], dst_ref=buf.at[1, j, rows], send_sem=xs.at[i], recv_sem=xr.at[i],
+            device_id={"wsh": across}, device_id_type=MESH,
+        )
+
+    def y_copy(i, side=None):
+        buf, j, s, half, step = place(i)
+        side = grp if side is None else side
+        rows = pl.ds(pl.multiple_of(side * half + s * step, 16), step)
+        return pltpu.make_async_remote_copy(
+            src_ref=buf.at[1, j, rows], dst_ref=buf.at[1, j, rows], send_sem=ys.at[i], recv_sem=yr.at[i],
+            device_id={"grp": 1 - grp}, device_id_type=MESH,
+        )
+
+    def forward(i):
+        x_copy(i).wait_recv()
+        y_copy(i).start()
+
+    loads[0].wait()
+    per = step_g // GROUP
+    for j in range(3):
+        for s in range(3):
+            expand(stage_g, fac_g, wg, j, grp * (half_g // GROUP) + s * per, per)
+            if j == 0 and s == 0:
+                pl.semaphore_wait(barrier, 9)
+            x_copy(j * 3 + s).start()
+
+    @pl.loop(0, tokens // 32)
+    def _(b):
+        rows = pl.ds(pl.multiple_of(b * 32, 32), 32)
+        values = hid[rows, :].astype(jnp.float32)
+        meansq = jnp.sum(values * values, axis=-1, keepdims=True) / depth
+        nrm[rows, :] = (values * lax.rsqrt(meansq + EPSILON) * gain[...]).astype(jnp.bfloat16)
+
+    picks = ids.shape[1]
+    chosen = ids[...]
+    gate_values = gates[...].astype(jnp.float32)
+    label = lax.broadcasted_iota(jnp.int32, (tokens, 128), 1)
+    named = jnp.zeros((tokens, 128), jnp.float32)
+    for k in range(picks):
+        named = named + jnp.where(chosen[:, k : k + 1] == label, 1.0, 0.0)
+    row_at = lax.broadcasted_iota(jnp.int32, (tokens, tokens), 0)
+    col_at = lax.broadcasted_iota(jnp.int32, (tokens, tokens), 1)
+    earlier = jnp.where(col_at < row_at, 1.0, 0.0).astype(jnp.bfloat16)
+    rank = jnp.dot(earlier, named.astype(jnp.bfloat16), preferred_element_type=jnp.float32)
+    blocks = []
+    weights = []
+    lane = lax.broadcasted_iota(jnp.int32, (tokens, 128), 1)
+    for pair in range(2):
+        expert = jnp.where(lane < cap, 2 * pair, 2 * pair + 1)
+        position = jnp.where(lane < cap, lane, lane - cap).astype(jnp.float32)
+        ranked = jnp.where(
+            lane < cap, rank[:, 2 * pair : 2 * pair + 1], rank[:, 2 * pair + 1 : 2 * pair + 2]
+        )
+        hit = jnp.zeros((tokens, 128), jnp.float32)
+        value = jnp.zeros((tokens, 128), jnp.float32)
+        for k in range(picks):
+            same = chosen[:, k : k + 1] == expert
+            hit = hit + jnp.where(same, 1.0, 0.0)
+            value = value + jnp.where(same, gate_values[:, k : k + 1], 0.0)
+        placed = jnp.where(ranked == position, hit, 0.0)
+        blocks.append(placed.T.astype(jnp.bfloat16))
+        weighting[:, pair * 128 : (pair + 1) * 128] = (placed * value).astype(jnp.bfloat16)
+    for pair in range(2):
+        rows = jnp.dot(blocks[pair], nrm[...], preferred_element_type=jnp.float32).astype(jnp.bfloat16)
+        og[2 * pair] = rows[:cap]
+        og[2 * pair + 1] = rows[cap:]
+
+    def slot_rows(s):
+        return pl.ds(pl.multiple_of(s * cap, 16), cap)
+
+    def z_copy(d):
+        to = (z + d) % 4
+        return pltpu.make_async_remote_copy(
+            src_ref=og.at[to], dst_ref=xb.at[slot_rows(slot)], send_sem=zs.at[d], recv_sem=zr.at[d],
+            device_id={"exp": to}, device_id_type=MESH,
+        )
+
+    def z_arrived(d):
+        frm = ((z + 4 - d) % 4) * 2 + c
+        pltpu.make_async_remote_copy(
+            src_ref=og.at[0], dst_ref=xb.at[slot_rows(frm)], send_sem=zs.at[d], recv_sem=zr.at[d],
+            device_id={"exp": (z + d) % 4}, device_id_type=MESH,
+        ).wait_recv()
+
+    def c_copy(d, core=None):
+        core = c if core is None else core
+        rows = slot_rows(((z + 4 - d) % 4) * 2 + core)
+        return pltpu.make_async_remote_copy(
+            src_ref=xb.at[rows], dst_ref=xb.at[rows], send_sem=cs.at[d], recv_sem=cr.at[d],
+            device_id={"wsh": mate}, device_id_type=MESH,
+        )
+
+    for d in (2, 1, 3):
+        z_copy(d).start()
+    xb[slot_rows(slot), :] = og[z]
+    c_copy(0).start()
+
+    loads[2].wait()
+    for j in range(3):
+        expand(stage_d, fac_d, wd, j, 0, inner // GROUP)
+        for s in range(3):
+            x_copy(9 + j * 3 + s).start()
+    loads[1].wait()
+    for j in range(3):
+        expand(stage_g, fac_g, wg, j, (1 - grp) * (half_g // GROUP), half_g // GROUP)
+
+    forward(0)
+    forward(1)
+    forward(2)
+    z_arrived(1)
+    c_copy(1).start()
+    z_arrived(3)
+    c_copy(3).start()
+    forward(3)
+    z_arrived(2)
+    c_copy(2).start()
+    forward(4)
+    for d in range(4):
+        c_copy(d, 1 - c).wait_recv()
+    for j in range(3):
+        first[j] = jnp.dot(xb[...], wg[0, j], preferred_element_type=jnp.float32)
+        forward(5 + j)
+    forward(8)
+
+    rows_all = xb.shape[0]
+    for j in range(3):
+        for s in range(3):
+            y_copy(j * 3 + s, 1 - grp).wait_recv()
+        second = jnp.dot(xb[...], wg[1, j], preferred_element_type=jnp.float32)
+        mine = first[j]
+        gate = jnp.where(x == 0, mine, second)
+        up = jnp.where(x == 0, second, mine)
+        done = ((up + 1.0) * gate * jax.nn.sigmoid(SWISH_ALPHA * gate)).astype(jnp.bfloat16)
+        lanes = min(TILE, width - j * TILE)
+        act[c, :, j * TILE : j * TILE + lanes] = done[:, :lanes]
+
+    def a_copy(core):
+        return pltpu.make_async_remote_copy(
+            src_ref=act.at[core], dst_ref=act.at[core], send_sem=act_s, recv_sem=act_r,
+            device_id={"wsh": mate}, device_id_type=MESH,
+        )
+
+    a_copy(c).start()
+    forward(9)
+    forward(10)
+    a_copy(1 - c).wait_recv()
+
+    def quarter(h, core):
+        return (x if h == 0 else 1 - x) * 2 + core
+
+    def r_copy(h, j, d):
+        other = (slot + d) % 8
+        q = quarter(h, c)
+        return pltpu.make_async_remote_copy(
+            src_ref=res.at[h, j, slot_rows(other)], dst_ref=back.at[q, j, slot_rows(z)],
+            send_sem=rs.at[h, j, d], recv_sem=rr.at[q, j, z],
+            device_id={"exp": other // 2, "wsh": x * 2 + other % 2}, device_id_type=MESH,
+        )
+
+    def project(h, j):
+        total = jnp.dot(act[0], wd[h, j, :half_d], preferred_element_type=jnp.float32)
+        total = total + jnp.dot(act[1], wd[h, j, half_d:], preferred_element_type=jnp.float32)
+        res[h, j] = total.astype(jnp.bfloat16)
+        for d in (4, 5, 2, 3, 6, 7, 1):
+            r_copy(h, j, d).start()
+        back[quarter(h, c), j, slot_rows(z), :] = res[h, j, slot_rows(slot), :]
+
+    def combine(h, j):
+        for core in range(2):
+            q = quarter(h, core)
+            for e in range(4):
+                @pl.when(jnp.logical_or(core != c, e != z))
+                def _():
+                    pltpu.make_async_remote_copy(
+                        src_ref=res.at[h, j, slot_rows(0)], dst_ref=back.at[q, j, slot_rows(e)],
+                        send_sem=rs.at[h, j, 1], recv_sem=rr.at[q, j, e],
+                        device_id={"wsh": mate}, device_id_type=MESH,
+                    ).wait_recv()
+            out[q, :, j * TILE : (j + 1) * TILE] = jnp.dot(
+                weighting[...], back[q, j], preferred_element_type=jnp.float32
+            ).astype(jnp.bfloat16)
+
+    project(0, 0)
+    forward(11)
+    project(0, 1)
+    forward(12)
+    project(0, 2)
+    forward(13)
+    for j in range(3):
+        for i in range(14 + 3 * j, min(17 + 3 * j, 18)):
+            forward(i)
+        for s in range(3):
+            y_copy(9 + j * 3 + s, 1 - grp).wait_recv()
+        project(1, j)
+        if j > 0:
+            combine(0, j - 1)
+    combine(0, 2)
+    for j in range(3):
+        combine(1, j)
+
+    for i in range(18):
+        x_copy(i).wait_send()
+        y_copy(i).wait_send()
+    for d in range(4):
+        if d > 0:
+            z_copy(d).wait_send()
+        c_copy(d).wait_send()
+    a_copy(c).wait_send()
+    for h in range(2):
+        for j in range(3):
+            for d in range(1, 8):
+                r_copy(h, j, d).wait_send()
+
+
+def fused_device(
+    hidden_in,
+    norm_gain,
+    expert_ids,
+    gate_weights,
+    gate_up_codes,
+    gate_up_scales,
+    down_codes,
+    down_scales,
+):
+    tokens, depth = hidden_in.shape
+    width = gate_up_codes.shape[2]
+    inner = down_codes.shape[1]
+    owners = lax.axis_size("exp")
+    cap = min(tokens // 2, tokens * expert_ids.shape[1] // owners)
+    rows = 2 * owners * cap
+    vmem = pl.BlockSpec(memory_space=pltpu.VMEM)
+    hbm = pl.BlockSpec(memory_space=pl.ANY)
+    bf16, f32 = jnp.bfloat16, jnp.float32
+    dma = pltpu.SemaphoreType.DMA
+    tiles = pl.cdiv(width, TILE)
+    out = pl.pallas_call(
+        fused_kernel,
+        out_shape=jax.ShapeDtypeStruct((4, tokens, tiles * TILE), bf16),
+        in_specs=[vmem, vmem, vmem, vmem, hbm, vmem, hbm, vmem],
+        out_specs=vmem,
+        scratch_shapes=[
+            pltpu.VMEM((depth, width), bf16),
+            pltpu.VMEM((inner, width), bf16),
+            pltpu.VMEM(gate_up_scales.shape[1:], f32),
+            pltpu.VMEM(down_scales.shape[1:], f32),
+            pltpu.VMEM((2, tiles, depth, TILE), bf16),
+            pltpu.VMEM((2, tiles, inner, TILE), bf16),
+            pltpu.VMEM((tokens, depth), bf16),
+            pltpu.VMEM((tokens, owners * cap), bf16),
+            pltpu.VMEM((owners, cap, depth), bf16),
+            pltpu.VMEM((rows, depth), bf16),
+            pltpu.VMEM((tiles, rows, TILE), f32),
+            pltpu.VMEM((2, rows, width), bf16),
+            pltpu.VMEM((2, tiles, rows, TILE), bf16),
+            pltpu.VMEM((4, tiles, owners * cap, TILE), bf16),
+            dma((3,)),
+            dma((18,)), dma((18,)), dma((18,)), dma((18,)),
+            dma((4,)), dma((4,)), dma((4,)), dma((4,)),
+            dma, dma,
+            dma((2, tiles, 8)), dma((4, tiles, owners)),
+        ],
+        compiler_params=pltpu.CompilerParams(
+            collective_id=0, has_side_effects=True, vmem_limit_bytes=58 * 1024 * 1024
+        ),
+        name="moe_block",
+    )(
+        hidden_in,
+        norm_gain.reshape(1, depth),
+        expert_ids,
+        gate_weights,
+        gate_up_codes,
+        gate_up_scales,
+        down_codes,
+        down_scales,
+    )
+    return jnp.concatenate([out[q, :, :width] for q in range(4)], axis=1)
+
+
 def solution(mesh):
     placed = (
         P(("grp", "exp", "wsh"), None),
@@ -97,8 +447,11 @@
         P("exp", None, "wsh"),
         P("exp", None, "wsh"),
     )
+    body = per_device
+    if mesh.shape["wsh"] == 4 and mesh.shape["exp"] == 4 and mesh.shape["grp"] == 2:
+        body = fused_device
     return jax.shard_map(
-        per_device,
+        body,
         mesh=mesh,
         in_specs=placed,
         out_specs=P(("grp", "exp", "wsh"), None),

time: 375 us -> 134 us (0.36)
  waiting for transfers between devices: 174 us -> 0 us
  Pallas kernels: 0 us -> 115 us
  local copies, waits for them, and re-layouts: 83.9 us -> 19.2 us
  blocking collectives: 40.2 us -> 0 us
  matrix products: 25.2 us -> 0 us
  other arithmetic: 24.9 us -> 0 us
  between operations: 13.6 us -> 0.02 us
  starting transfers between devices: 11.2 us -> 0 us
    all_gather x2 -> x0, waiting for transfers between devices: 137 us -> none  [the longest x1 72.4 us: per_device(): lax.all_gather((down_codes[0], down_scales[0]), 'wsh', axis=1, tiled=True)]
    pallas_call x0 -> x1, Pallas kernels: none -> 115 us  [fused_device(): pl.pallas_call(fused_kernel, out_shape=jax.ShapeDtypeStruct((4, tokens, t...]
    all_gather x4 -> x0, local copies, waits for them, and re-layouts: 65.8 us -> none  [the longest x2 40.4 us: per_device(): lax.all_gather((down_codes[0], down_scales[0]), 'wsh', axis=1, tiled=True)]
    all_gather x2 -> x0, blocking collectives: 40.2 us -> none  [the longest x1 20.7 us: per_device(): lax.all_gather((gate_up_codes[0], gate_up_scales[0]), 'wsh', axis=1, tile...]
    all_to_all x2 -> x0, waiting for transfers between devices: 35.8 us -> none  [the longest x1 35.8 us: per_device(): lax.all_to_all(expert_rows, 'exp', split_axis=0, concat_axis=0, tiled=True)]
    dot_general x4 -> x0, matrix products: 25.2 us -> none  [the longest x1 14.9 us: per_device(): jnp.dot(arrived, expand_block(shard_piece[0], shard_piece[1]), preferred_...]
    mul x3 -> x0, other arithmetic: 22.4 us -> none  [the longest x2 22.4 us: expand_block(): return (shaped * factor[..., :, None, :]).reshape(mantissa.shape)]
    all_to_all x2 -> x0, starting transfers between devices: 11.2 us -> none  [the longest x1 6.45 us: per_device(): lax.all_to_all(outgoing, 'exp', split_axis=0, concat_axis=0, tiled=True)]
  transfers between devices with their start and end apart: 4 -> 0, of which waited for: 3 -> 0; matrix products, arithmetic and copies ran while one was open for 26% -> 0% of each run, Pallas kernels for 0% -> 0%
where the time goes in v1:
time: 134 us
  Pallas kernels  115 us (86%)
  local copies, waits for them, and re-layouts  19.2 us (14%)
    pallas_call x1, Pallas kernels, fused_device(): pl.pallas_call(fused_kernel, out_shape=jax.ShapeDtypeStruct((4, tokens, t...  115 us
    unnamed x6, local copies, waits for them, and re-layouts  14.9 us

profile of v1, /device:TPU:0, one launch (start us, length us, event | category | flops | bytes accessed | tf_op | source)
XLA Modules:
  0.0 133.8 jit_solution(12319958121595311909)
XLA Ops:
  0.0 1.3 reshape.3.gain
  1.3 1.4 %copy.11.gates = bf16[128,4]{1,0:T(8,128)(2,1)} copy(bf16[128,4]{0,1:T(4,128)(2,1)} %param.11) | data formatting | bytes 2048 | tf_op args[3]
  2.7 1.4 %copy.10.ids = s32[128,4]{1,0:T(8,128)} copy(s32[128,4]{0,1:T(4,128)} %param.10) | data formatting | bytes 4096 | tf_op args[2]
  4.1 1.6 %copy.14.dns = s32[1,45,720]{2,1,0:T(8,128)} copy(s32[1,45,720]{2,0,1:T(1,128)} %param.15) | data formatting | bytes 259200 | tf_op args[7]
  5.7 1.7 %copy.13.gus = s32[1,90,720]{2,1,0:T(8,128)} copy(s32[1,90,720]{2,0,1:T(1,128)} %param.13) | data formatting | bytes 518400 | tf_op args[5]
  7.4 2.3 %copy.9.hid = bf16[128,2880]{1,0:T(8,128)(2,1)} copy(bf16[128,2880]{0,1:T(8,128)(2,1)} %param.8) | data formatting | bytes 1474560 | tf_op args[0]
  9.7 6.5 %copy.12.guc = bf16[1,2880,720]{2,1,0:T(8,128)(2,1)} copy(bf16[1,2880,720]{1,2,0:T(8,128)(2,1)} %param.12) | data formatting | bytes 8294400 | tf_op args[4]
  16.2 114.6 %moe_block.1 = bf16[4,128,768]{2,1,0:T(8,128)(2,1)} custom-call(bf16[128,2880]{1,0:T(8,128)(2,1)} %copy.9.hid, f32[1,2880]{1,0:T(1,128)} %reshape.3.gain, s32[128,4]{1,0:T(8,128)} %copy.10.ids, bf16[128,4]{1,0:T(8,128)(2,1)} %copy.11.gates, bf16[1,2880,720]{2,1,0:T(8,128)(2,1)} %copy.12.guc, s32[1,90,720]{2,1,0:T(8,128)} %copy.13.gus, ...), custom_call_target="tpu_custom_call" | custom-call | tf_op jit(solution)/shard_map/moe_block/pallas_call | solution.py:396
  130.8 1.3 slice_bitcast_fusion
  132.1 0.6 concatenate.3
  132.7 1.1 copy.15

commit v2 on v1

--- a/solution.py
+++ b/solution.py
@@ -95,7 +95,7 @@
 
 def fused_kernel(
     hid, gain, ids, gates, guc, gus, dnc, dns, out,
-    stage_g, stage_d, fac_g, fac_d, wg, wd, nrm, weighting, og, xb, first, act, res, back,
+    stage_g, stage_d, wg, wd, nrm, weighting, og, xb, first, act, res, back,
     load_sem, xs, xr, ys, yr, zs, zr, cs, cr, act_s, act_r, rs, rr,
 ):
     grp = lax.axis_index("grp")
@@ -106,19 +106,21 @@
     slot = z * 2 + c
     mate = x * 2 + (1 - c)
     across = (1 - x) * 2 + c
-    depth, width = stage_g.shape
-    inner = stage_d.shape[0]
+    depth = stage_g.shape[1]
+    inner, width = stage_d.shape
     half_g, half_d = depth // 2, inner // 2
-    step_g, step_d = half_g // 3, half_d // 3
-    tokens = hid.shape[0]
+    per_g, per_d = 6, 3
+    step_g, step_d = half_g // per_g, half_d // per_d
+    count_g = 3 * per_g
+    count = count_g + 3 * per_d
+    tokens = hid.shape[1]
     cap = og.shape[1]
 
     loads = []
-    for k in range(2):
-        part = (grp + k) % 2
-        rows = pl.ds(pl.multiple_of(part * half_g, 16), half_g)
-        loads.append(pltpu.make_async_copy(guc.at[0, rows], stage_g.at[rows], load_sem.at[k]))
-    loads.append(pltpu.make_async_copy(dnc.at[0], stage_d, load_sem.at[2]))
+    for j in range(3):
+        rows = pl.ds(j * TILE, min(TILE, width - j * TILE))
+        loads.append(pltpu.make_async_copy(guc.at[0, rows], stage_g.at[rows], load_sem.at[j]))
+    loads.append(pltpu.make_async_copy(dnc.at[0], stage_d, load_sem.at[3]))
     for load in loads:
         load.start()
 
@@ -131,28 +133,46 @@
             barrier, inc=1, device_id={"exp": other // 2, "wsh": x * 2 + other % 2}, device_id_type=MESH
         )
 
-    fac_g[...] = jnp.exp2(-gus[0].astype(jnp.float32))
-    fac_d[...] = jnp.exp2(-dns[0].astype(jnp.float32))
     wg[0, 2] = jnp.zeros((depth, TILE), jnp.bfloat16)
     wd[0, 2] = jnp.zeros((inner, TILE), jnp.bfloat16)
-
-    def expand(stage, fac, dest, j, start, groups):
+    stage_g[width:, :] = jnp.zeros((stage_g.shape[0] - width, depth), jnp.bfloat16)
+
+    def factor(scales, at, j, lanes):
+        scale = jnp.exp2(-scales[at, :, pl.ds(j * TILE, lanes)].astype(jnp.float32))
+        return jnp.broadcast_to(scale, (GROUP, lanes)).astype(jnp.bfloat16)
+
+    def expand_down(j):
         lanes = min(TILE, width - j * TILE)
 
-        @pl.loop(0, groups)
+        @pl.loop(0, inner // GROUP)
         def _(g):
-            at = start + g
-            row = pl.multiple_of(at * GROUP, GROUP)
-            scale = fac[pl.ds(at, 1), pl.ds(j * TILE, lanes)]
-            scale = jnp.broadcast_to(scale, (GROUP, lanes)).astype(jnp.bfloat16)
-            dest[0, j, pl.ds(row, GROUP), pl.ds(0, lanes)] = (
-                stage[pl.ds(row, GROUP), pl.ds(j * TILE, lanes)] * scale
-            )
+            row = pl.multiple_of(g * GROUP, GROUP)
+            wd[0, j, pl.ds(row, GROUP), pl.ds(0, lanes)] = stage_d[
+                pl.ds(row, GROUP), pl.ds(j * TILE, lanes)
+            ] * factor(dns, g, j, lanes)
+
+    def expand_gate_up(j):
+        lanes = min(TILE, width - j * TILE)
+
+        def block(at, extent):
+            codes = stage_g[pl.ds(j * TILE, TILE), pl.ds(at, extent)].T
+            for g in range(extent // GROUP):
+                part = codes[g * GROUP : (g + 1) * GROUP, :lanes]
+                scale = factor(gus, at // GROUP + g, j, lanes)
+                wg[0, j, pl.ds(at + g * GROUP, GROUP), pl.ds(0, lanes)] = part * scale
+
+        @pl.loop(0, depth // 128)
+        def _(b):
+            block(pl.multiple_of(b * 128, 128), 128)
+
+        if depth % 128:
+            block(depth // 128 * 128, depth % 128)
 
     def place(i):
-        buf = wg if i < 9 else wd
-        j, s = (i % 9) // 3, i % 3
-        return buf, j, s, (half_g if i < 9 else half_d), (step_g if i < 9 else step_d)
+        if i < count_g:
+            return wg, i // per_g, i % per_g, half_g, step_g
+        i = i - count_g
+        return wd, i // per_d, i % per_d, half_d, step_d
 
     def x_copy(i):
         buf, j, s, half, step = place(i)
@@ -175,55 +195,53 @@
         x_copy(i).wait_recv()
         y_copy(i).start()
 
-    loads[0].wait()
-    per = step_g // GROUP
-    for j in range(3):
-        for s in range(3):
-            expand(stage_g, fac_g, wg, j, grp * (half_g // GROUP) + s * per, per)
-            if j == 0 and s == 0:
-                pl.semaphore_wait(barrier, 9)
-            x_copy(j * 3 + s).start()
-
-    @pl.loop(0, tokens // 32)
-    def _(b):
-        rows = pl.ds(pl.multiple_of(b * 32, 32), 32)
-        values = hid[rows, :].astype(jnp.float32)
-        meansq = jnp.sum(values * values, axis=-1, keepdims=True) / depth
-        nrm[rows, :] = (values * lax.rsqrt(meansq + EPSILON) * gain[...]).astype(jnp.bfloat16)
-
-    picks = ids.shape[1]
+    for j in range(3):
+        loads[j].wait()
+        expand_gate_up(j)
+        if j == 0:
+            pl.semaphore_wait(barrier, 9)
+        for s in range(per_g):
+            x_copy(j * per_g + s).start()
+
+    total = jnp.zeros((1, tokens), jnp.float32)
+    for at in range(0, depth, 128):
+        values = hid[at : min(at + 128, depth), :].astype(jnp.float32)
+        total = total + jnp.sum(values * values, axis=0, keepdims=True)
+    inverse = lax.rsqrt(total / depth + EPSILON)
+    for at in range(0, depth, 128):
+        end = min(at + 128, depth)
+        values = (hid[at:end, :].astype(jnp.float32) * inverse).T
+        nrm[:, at:end] = (values * gain[:, at:end]).astype(jnp.bfloat16)
+
+    picks = ids.shape[0]
+    owners = og.shape[0]
     chosen = ids[...]
     gate_values = gates[...].astype(jnp.float32)
-    label = lax.broadcasted_iota(jnp.int32, (tokens, 128), 1)
-    named = jnp.zeros((tokens, 128), jnp.float32)
+    label = lax.broadcasted_iota(jnp.int32, (16, tokens), 0)
+    named = jnp.zeros((16, tokens), jnp.float32)
+    valued = jnp.zeros((16, tokens), jnp.float32)
     for k in range(picks):
-        named = named + jnp.where(chosen[:, k : k + 1] == label, 1.0, 0.0)
+        same = chosen[k : k + 1, :] == label
+        named = named + jnp.where(same, 1.0, 0.0)
+        valued = valued + jnp.where(same, gate_values[k : k + 1, :], 0.0)
     row_at = lax.broadcasted_iota(jnp.int32, (tokens, tokens), 0)
     col_at = lax.broadcasted_iota(jnp.int32, (tokens, tokens), 1)
-    earlier = jnp.where(col_at < row_at, 1.0, 0.0).astype(jnp.bfloat16)
-    rank = jnp.dot(earlier, named.astype(jnp.bfloat16), preferred_element_type=jnp.float32)
-    blocks = []
-    weights = []
-    lane = lax.broadcasted_iota(jnp.int32, (tokens, 128), 1)
-    for pair in range(2):
-        expert = jnp.where(lane < cap, 2 * pair, 2 * pair + 1)
-        position = jnp.where(lane < cap, lane, lane - cap).astype(jnp.float32)
-        ranked = jnp.where(
-            lane < cap, rank[:, 2 * pair : 2 * pair + 1], rank[:, 2 * pair + 1 : 2 * pair + 2]
-        )
-        hit = jnp.zeros((tokens, 128), jnp.float32)
-        value = jnp.zeros((tokens, 128), jnp.float32)
-        for k in range(picks):
-            same = chosen[:, k : k + 1] == expert
-            hit = hit + jnp.where(same, 1.0, 0.0)
-            value = value + jnp.where(same, gate_values[:, k : k + 1], 0.0)
-        placed = jnp.where(ranked == position, hit, 0.0)
-        blocks.append(placed.T.astype(jnp.bfloat16))
-        weighting[:, pair * 128 : (pair + 1) * 128] = (placed * value).astype(jnp.bfloat16)
-    for pair in range(2):
-        rows = jnp.dot(blocks[pair], nrm[...], preferred_element_type=jnp.float32).astype(jnp.bfloat16)
-        og[2 * pair] = rows[:cap]
-        og[2 * pair + 1] = rows[cap:]
+    earlier = jnp.where(row_at < col_at, 1.0, 0.0).astype(jnp.bfloat16)
+    rank = jnp.dot(named.astype(jnp.bfloat16), earlier, preferred_element_type=jnp.float32)
+    position = lax.broadcasted_iota(jnp.int32, (cap, tokens), 0).astype(jnp.float32)
+    placed = []
+    for e in range(owners):
+        hit = jnp.where(rank[e : e + 1, :] == position, named[e : e + 1, :], 0.0)
+        placed.append(hit)
+        og[e] = jnp.dot(
+            hit.astype(jnp.bfloat16), nrm[...], preferred_element_type=jnp.float32
+        ).astype(jnp.bfloat16)
+    for pair in range(owners // 2):
+        e = 2 * pair
+        both = jnp.concatenate(
+            [placed[e] * valued[e : e + 1, :], placed[e + 1] * valued[e + 1 : e + 2, :]], axis=0
+        )
+        weighting[:, 2 * cap * pair : 2 * cap * (pair + 1)] = both.T.astype(jnp.bfloat16)
 
     def slot_rows(s):
         return pl.ds(pl.multiple_of(s * cap, 16), cap)
@@ -255,55 +273,47 @@
     xb[slot_rows(slot), :] = og[z]
     c_copy(0).start()
 
-    loads[2].wait()
-    for j in range(3):
-        expand(stage_d, fac_d, wd, j, 0, inner // GROUP)
-        for s in range(3):
-            x_copy(9 + j * 3 + s).start()
-    loads[1].wait()
-    for j in range(3):
-        expand(stage_g, fac_g, wg, j, (1 - grp) * (half_g // GROUP), half_g // GROUP)
-
-    forward(0)
-    forward(1)
-    forward(2)
-    z_arrived(1)
-    c_copy(1).start()
-    z_arrived(3)
-    c_copy(3).start()
-    forward(3)
-    z_arrived(2)
-    c_copy(2).start()
-    forward(4)
+    loads[3].wait()
+    for j in range(3):
+        expand_down(j)
+        for s in range(per_d):
+            x_copy(count_g + j * per_d + s).start()
+    for i in range(12):
+        forward(i)
+    for d in (1, 3, 2):
+        z_arrived(d)
+        c_copy(d).start()
+    forward(12)
     for d in range(4):
         c_copy(d, 1 - c).wait_recv()
-    for j in range(3):
-        first[j] = jnp.dot(xb[...], wg[0, j], preferred_element_type=jnp.float32)
-        forward(5 + j)
-    forward(8)
-
-    rows_all = xb.shape[0]
-    for j in range(3):
-        for s in range(3):
-            y_copy(j * 3 + s, 1 - grp).wait_recv()
+
+    def a_copy(core, j):
+        return pltpu.make_async_remote_copy(
+            src_ref=act.at[core, j], dst_ref=act.at[core, j], send_sem=act_s.at[j], recv_sem=act_r.at[j],
+            device_id={"wsh": mate}, device_id_type=MESH,
+        )
+
+    def activate_tile(j):
+        for s in range(per_g):
+            y_copy(j * per_g + s, 1 - grp).wait_recv()
         second = jnp.dot(xb[...], wg[1, j], preferred_element_type=jnp.float32)
         mine = first[j]
         gate = jnp.where(x == 0, mine, second)
         up = jnp.where(x == 0, second, mine)
-        done = ((up + 1.0) * gate * jax.nn.sigmoid(SWISH_ALPHA * gate)).astype(jnp.bfloat16)
-        lanes = min(TILE, width - j * TILE)
-        act[c, :, j * TILE : j * TILE + lanes] = done[:, :lanes]
-
-    def a_copy(core):
-        return pltpu.make_async_remote_copy(
-            src_ref=act.at[core], dst_ref=act.at[core], send_sem=act_s, recv_sem=act_r,
-            device_id={"wsh": mate}, device_id_type=MESH,
-        )
-
-    a_copy(c).start()
-    forward(9)
-    forward(10)
-    a_copy(1 - c).wait_recv()
+        act[c, j] = ((up + 1.0) * gate * jax.nn.sigmoid(SWISH_ALPHA * gate)).astype(jnp.bfloat16)
+        a_copy(c, j).start()
+
+    for j in range(3):
+        first[j] = jnp.dot(xb[...], wg[0, j], preferred_element_type=jnp.float32)
+        forward(13 + j)
+    activate_tile(0)
+    forward(16)
+    activate_tile(1)
+    forward(17)
+    activate_tile(2)
+    forward(count_g)
+    for j in range(3):
+        a_copy(1 - c, j).wait_recv()
 
     def quarter(h, core):
         return (x if h == 0 else 1 - x) * 2 + core
@@ -318,8 +328,14 @@
         )
 
     def project(h, j):
-        total = jnp.dot(act[0], wd[h, j, :half_d], preferred_element_type=jnp.float32)
-        total = total + jnp.dot(act[1], wd[h, j, half_d:], preferred_element_type=jnp.float32)
+        total = jnp.zeros((act.shape[2], TILE), jnp.float32)
+        for core in range(2):
+            for k in range(3):
+                lanes = min(TILE, width - k * TILE)
+                at = core * half_d + k * TILE
+                total = total + jnp.dot(
+                    act[core, k, :, :lanes], wd[h, j, at : at + lanes], preferred_element_type=jnp.float32
+                )
         res[h, j] = total.astype(jnp.bfloat16)
         for d in (4, 5, 2, 3, 6, 7, 1):
             r_copy(h, j, d).start()
@@ -336,21 +352,21 @@
                         send_sem=rs.at[h, j, 1], recv_sem=rr.at[q, j, e],
                         device_id={"wsh": mate}, device_id_type=MESH,
                     ).wait_recv()
-            out[q, :, j * TILE : (j + 1) * TILE] = jnp.dot(
-                weighting[...], back[q, j], preferred_element_type=jnp.float32
-            ).astype(jnp.bfloat16)
+            mixed = jnp.dot(weighting[...], back[q, j], preferred_element_type=jnp.float32)
+            lanes = min(TILE, width - j * TILE)
+            at = pl.multiple_of(q * width + j * TILE, 16)
+            out[pl.ds(at, lanes), :] = mixed.T[:lanes].astype(jnp.bfloat16)
 
     project(0, 0)
-    forward(11)
+    forward(count_g + 1)
     project(0, 1)
-    forward(12)
+    forward(count_g + 2)
     project(0, 2)
-    forward(13)
-    for j in range(3):
-        for i in range(14 + 3 * j, min(17 + 3 * j, 18)):
+    for j in range(3):
+        for i in range(count_g + 3 + 3 * j, min(count_g + 6 + 3 * j, count)):
             forward(i)
-        for s in range(3):
-            y_copy(9 + j * 3 + s, 1 - grp).wait_recv()
+        for s in range(per_d):
+            y_copy(count_g + j * per_d + s, 1 - grp).wait_recv()
         project(1, j)
         if j > 0:
             combine(0, j - 1)
@@ -358,14 +374,15 @@
     for j in range(3):
         combine(1, j)
 
-    for i in range(18):
+    for i in range(count):
         x_copy(i).wait_send()
         y_copy(i).wait_send()
     for d in range(4):
         if d > 0:
             z_copy(d).wait_send()
         c_copy(d).wait_send()
-    a_copy(c).wait_send()
+    for j in range(3):
+        a_copy(c, j).wait_send()
     for h in range(2):
         for j in range(3):
             for d in range(1, 8):
@@ -395,14 +412,12 @@
     tiles = pl.cdiv(width, TILE)
     out = pl.pallas_call(
         fused_kernel,
-        out_shape=jax.ShapeDtypeStruct((4, tokens, tiles * TILE), bf16),
+        out_shape=jax.ShapeDtypeStruct((depth, tokens), bf16),
         in_specs=[vmem, vmem, vmem, vmem, hbm, vmem, hbm, vmem],
         out_specs=vmem,
         scratch_shapes=[
-            pltpu.VMEM((depth, width), bf16),
+            pltpu.VMEM((tiles * TILE, depth), bf16),
             pltpu.VMEM((inner, width), bf16),
-            pltpu.VMEM(gate_up_scales.shape[1:], f32),
-            pltpu.VMEM(down_scales.shape[1:], f32),
             pltpu.VMEM((2, tiles, depth, TILE), bf16),
             pltpu.VMEM((2, tiles, inner, TILE), bf16),
             pltpu.VMEM((tokens, depth), bf16),
@@ -410,13 +425,13 @@
             pltpu.VMEM((owners, cap, depth), bf16),
             pltpu.VMEM((rows, depth), bf16),
             pltpu.VMEM((tiles, rows, TILE), f32),
-            pltpu.VMEM((2, rows, width), bf16),
+            pltpu.VMEM((2, tiles, rows, TILE), bf16),
             pltpu.VMEM((2, tiles, rows, TILE), bf16),
             pltpu.VMEM((4, tiles, owners * cap, TILE), bf16),
-            dma((3,)),
-            dma((18,)), dma((18,)), dma((18,)), dma((18,)),
+            dma((4,)),
+            dma((27,)), dma((27,)), dma((27,)), dma((27,)),
             dma((4,)), dma((4,)), dma((4,)), dma((4,)),
-            dma, dma,
+            dma((3,)), dma((3,)),
             dma((2, tiles, 8)), dma((4, tiles, owners)),
         ],
         compiler_params=pltpu.CompilerParams(
@@ -424,16 +439,16 @@
         ),
         name="moe_block",
     )(
-        hidden_in,
+        hidden_in.T,
         norm_gain.reshape(1, depth),
-        expert_ids,
-        gate_weights,
-        gate_up_codes,
-        gate_up_scales,
+        expert_ids.T,
+        gate_weights.T,
+        jnp.swapaxes(gate_up_codes, 1, 2),
+        jnp.swapaxes(gate_up_scales, 0, 1),
         down_codes,
-        down_scales,
-    )
-    return jnp.concatenate([out[q, :, :width] for q in range(4)], axis=1)
+        jnp.swapaxes(down_scales, 0, 1),
+    )
+    return out.T
 
 
 def solution(mesh):

time: 134 us -> 110 us (0.82)
  local copies, waits for them, and re-layouts: 19.2 us -> 3.34 us
  Pallas kernels: 115 us -> 106 us
    unnamed x6 -> x1, local copies, waits for them, and re-layouts: 14.9 us -> 2.03 us
    pallas_call x1, Pallas kernels: 115 us -> 106 us  [fused_device(): pl.pallas_call(fused_kernel, out_shape=jax.ShapeDtypeStruct((depth, token...]
    concatenate x2 -> x0, local copies, waits for them, and re-layouts: 1.74 us -> none  [fused_device(): return jnp.concatenate([out[q, :, :width] for q in range(4)], axis=1)]
where the time goes in v2:
time: 110 us
  Pallas kernels  106 us (96%)
  local copies, waits for them, and re-layouts  3.34 us (3%)
    pallas_call x1, Pallas kernels, fused_device(): pl.pallas_call(fused_kernel, out_shape=jax.ShapeDtypeStruct((depth, token...  106 us

profile of v2, /device:TPU:0, one launch (start us, length us, event | category | flops | bytes accessed | tf_op | source)
XLA Modules:
  0.0 109.8 jit_solution(10095809750626096686)
XLA Ops:
  0.0 1.3 %reshape.3.gain = f32[1,2880]{1,0:T(1,128)} reshape(f32[2880]{0:T(1024)} %param.9) | data formatting | bytes 23040 | tf_op jit(solution)/shard_map/reshape | solution.py:443
  1.3 106.4 %moe_block.1 = bf16[2880,128]{1,0:T(8,128)(2,1)} custom-call(bf16[2880,128]{1,0:T(8,128)(2,1)} %bitcast.9, f32[1,2880]{1,0:T(1,128)} %reshape.3.gain, s32[4,128]{1,0:T(4,128)} %bitcast.12, bf16[4,128]{1,0:T(4,128)(2,1)} %bitcast.13, bf16[1,720,2880]{2,1,0:T(8,128)(2,1)} %bitcast.7, s32[90,1,720]{2,1,0:T(1,128)} %bitcast.10, bf16[1,1440,720]{2,1,0:T(8,128)(2,1)} %dnc.1, ...), custom_call_target="tpu_custom_call" | custom-call | tf_op jit(solution)/shard_map/moe_block/pallas_call | solution.py:413
  107.8 2.0 %copy.10 = bf16[128,2880]{0,1:T(8,128)(2,1)} copy(bf16[128,2880]{0,1:T(8,128)(2,1)} %bitcast.8) | data formatting | bytes 1474560

commit v3 on v2

--- a/solution.py
+++ b/solution.py
@@ -109,7 +109,7 @@
     depth = stage_g.shape[1]
     inner, width = stage_d.shape
     half_g, half_d = depth // 2, inner // 2
-    per_g, per_d = 6, 3
+    per_g, per_d = 9, 5
     step_g, step_d = half_g // per_g, half_d // per_d
     count_g = 3 * per_g
     count = count_g + 3 * per_d
@@ -195,13 +195,15 @@
         x_copy(i).wait_recv()
         y_copy(i).start()
 
-    for j in range(3):
+    def send_gate_up(j):
         loads[j].wait()
         expand_gate_up(j)
         if j == 0:
             pl.semaphore_wait(barrier, 9)
         for s in range(per_g):
             x_copy(j * per_g + s).start()
+
+    send_gate_up(0)
 
     total = jnp.zeros((1, tokens), jnp.float32)
     for at in range(0, depth, 128):
@@ -211,7 +213,7 @@
     for at in range(0, depth, 128):
         end = min(at + 128, depth)
         values = (hid[at:end, :].astype(jnp.float32) * inverse).T
-        nrm[:, at:end] = (values * gain[:, at:end]).astype(jnp.bfloat16)
+        nrm[:, at:end] = (values * gain[at:end].reshape(1, end - at)).astype(jnp.bfloat16)
 
     picks = ids.shape[0]
     owners = og.shape[0]
@@ -273,17 +275,23 @@
     xb[slot_rows(slot), :] = og[z]
     c_copy(0).start()
 
+    forward(0)
+    send_gate_up(1)
+    forward(1)
+    send_gate_up(2)
+    forward(2)
     loads[3].wait()
     for j in range(3):
         expand_down(j)
         for s in range(per_d):
             x_copy(count_g + j * per_d + s).start()
-    for i in range(12):
+        forward(3 + j)
+    for i in range(6, 21):
         forward(i)
     for d in (1, 3, 2):
         z_arrived(d)
         c_copy(d).start()
-    forward(12)
+    forward(21)
     for d in range(4):
         c_copy(d, 1 - c).wait_recv()
 
@@ -305,13 +313,14 @@
 
     for j in range(3):
         first[j] = jnp.dot(xb[...], wg[0, j], preferred_element_type=jnp.float32)
-        forward(13 + j)
+        forward(22 + j)
     activate_tile(0)
-    forward(16)
+    forward(25)
     activate_tile(1)
-    forward(17)
+    forward(26)
+    forward(27)
     activate_tile(2)
-    forward(count_g)
+    forward(28)
     for j in range(3):
         a_copy(1 - c, j).wait_recv()
 
@@ -357,20 +366,17 @@
             at = pl.multiple_of(q * width + j * TILE, 16)
             out[pl.ds(at, lanes), :] = mixed.T[:lanes].astype(jnp.bfloat16)
 
-    project(0, 0)
-    forward(count_g + 1)
-    project(0, 1)
-    forward(count_g + 2)
-    project(0, 2)
-    for j in range(3):
-        for i in range(count_g + 3 + 3 * j, min(count_g + 6 + 3 * j, count)):
+    for j in range(3):
+        project(0, j)
+        forward(29 + j)
+    for j in range(3):
+        for i in range(max(32, count_g + per_d * j), count_g + per_d * (j + 1)):
             forward(i)
         for s in range(per_d):
             y_copy(count_g + j * per_d + s, 1 - grp).wait_recv()
         project(1, j)
-        if j > 0:
-            combine(0, j - 1)
-    combine(0, 2)
+    for j in range(3):
+        combine(0, j)
     for j in range(3):
         combine(1, j)
 
@@ -429,7 +435,7 @@
             pltpu.VMEM((2, tiles, rows, TILE), bf16),
             pltpu.VMEM((4, tiles, owners * cap, TILE), bf16),
             dma((4,)),
-            dma((27,)), dma((27,)), dma((27,)), dma((27,)),
+            dma((42,)), dma((42,)), dma((42,)), dma((42,)),
             dma((4,)), dma((4,)), dma((4,)), dma((4,)),
             dma((3,)), dma((3,)),
             dma((2, tiles, 8)), dma((4, tiles, owners)),
@@ -440,7 +446,7 @@
         name="moe_block",
     )(
         hidden_in.T,
-        norm_gain.reshape(1, depth),
+        norm_gain,
         expert_ids.T,
         gate_weights.T,
         jnp.swapaxes(gate_up_codes, 1, 2),

time: 110 us -> 107 us (0.973)
  local copies, waits for them, and re-layouts: 3.34 us -> 2.03 us
    reshape x1 -> x0, local copies, waits for them, and re-layouts: 1.31 us -> none  [fused_device(): norm_gain.reshape(1, depth)]
    pallas_call x1, Pallas kernels: 106 us -> 105 us  [fused_device(): pl.pallas_call(fused_kernel, out_shape=jax.ShapeDtypeStruct((depth, token...]
where the time goes in v3:
time: 107 us
  Pallas kernels  105 us (98%)
  local copies, waits for them, and re-layouts  2.03 us (2%)
    pallas_call x1, Pallas kernels, fused_device(): pl.pallas_call(fused_kernel, out_shape=jax.ShapeDtypeStruct((depth, token...  105 us

profile of v3, /device:TPU:0, one launch (start us, length us, event | category | flops | bytes accessed | tf_op | source)
XLA Modules:
  0.0 107.2 jit_solution(7758692758382789665)
XLA Ops:
  0.0 105.2 %moe_block.1 = bf16[2880,128]{1,0:T(8,128)(2,1)} custom-call(bf16[2880,128]{1,0:T(8,128)(2,1)} %bitcast.9, f32[2880]{0:T(1024)} %gain.1, s32[4,128]{1,0:T(4,128)} %bitcast.12, bf16[4,128]{1,0:T(4,128)(2,1)} %bitcast.13, bf16[1,720,2880]{2,1,0:T(8,128)(2,1)} %bitcast.7, s32[90,1,720]{2,1,0:T(1,128)} %bitcast.10, bf16[1,1440,720]{2,1,0:T(8,128)(2,1)} %dnc.1, ...), custom_call_target="tpu_custom_call" | custom-call | tf_op jit(solution)/shard_map/moe_block/pallas_call | solution.py:419
  105.2 2.0 %copy.10 = bf16[128,2880]{0,1:T(8,128)(2,1)} copy(bf16[128,2880]{0,1:T(8,128)(2,1)} %bitcast.8) | data formatting | bytes 1474560

commit v4 on v3

--- a/solution.py
+++ b/solution.py
@@ -95,8 +95,8 @@
 
 def fused_kernel(
     hid, gain, ids, gates, guc, gus, dnc, dns, out,
-    stage_g, stage_d, wg, wd, nrm, weighting, og, xb, first, act, res, back,
-    load_sem, xs, xr, ys, yr, zs, zr, cs, cr, act_s, act_r, rs, rr,
+    stage_g, stage_d, wg, wd, og, xb, first, act, res, far, summed, back,
+    load_sem, xs, xr, ys, yr, zs, zr, cs, cr, act_s, act_r, rs, rr, fs, fr, ms,
 ):
     grp = lax.axis_index("grp")
     z = lax.axis_index("exp")
@@ -210,40 +210,25 @@
         values = hid[at : min(at + 128, depth), :].astype(jnp.float32)
         total = total + jnp.sum(values * values, axis=0, keepdims=True)
     inverse = lax.rsqrt(total / depth + EPSILON)
+    owners = og.shape[0]
     for at in range(0, depth, 128):
         end = min(at + 128, depth)
-        values = (hid[at:end, :].astype(jnp.float32) * inverse).T
-        nrm[:, at:end] = (values * gain[at:end].reshape(1, end - at)).astype(jnp.bfloat16)
+        values = (hid[at:end, :].astype(jnp.float32) * inverse).T[:cap]
+        rows = (values * gain[at:end].reshape(1, end - at)).astype(jnp.bfloat16)
+        for e in range(owners):
+            og[e, :, at:end] = rows
 
     picks = ids.shape[0]
-    owners = og.shape[0]
     chosen = ids[...]
     gate_values = gates[...].astype(jnp.float32)
-    label = lax.broadcasted_iota(jnp.int32, (16, tokens), 0)
-    named = jnp.zeros((16, tokens), jnp.float32)
-    valued = jnp.zeros((16, tokens), jnp.float32)
+    label = lax.broadcasted_iota(jnp.int32, (tokens, tokens), 0)
+    valued = jnp.zeros((tokens, tokens), jnp.float32)
     for k in range(picks):
-        same = chosen[k : k + 1, :] == label
-        named = named + jnp.where(same, 1.0, 0.0)
-        valued = valued + jnp.where(same, gate_values[k : k + 1, :], 0.0)
-    row_at = lax.broadcasted_iota(jnp.int32, (tokens, tokens), 0)
-    col_at = lax.broadcasted_iota(jnp.int32, (tokens, tokens), 1)
-    earlier = jnp.where(row_at < col_at, 1.0, 0.0).astype(jnp.bfloat16)
-    rank = jnp.dot(named.astype(jnp.bfloat16), earlier, preferred_element_type=jnp.float32)
-    position = lax.broadcasted_iota(jnp.int32, (cap, tokens), 0).astype(jnp.float32)
-    placed = []
+        valued = valued + jnp.where(chosen[k : k + 1, :] == label, gate_values[k : k + 1, :], 0.0)
+    valued = valued.T
+    spare = og.shape[2] - 128
     for e in range(owners):
-        hit = jnp.where(rank[e : e + 1, :] == position, named[e : e + 1, :], 0.0)
-        placed.append(hit)
-        og[e] = jnp.dot(
-            hit.astype(jnp.bfloat16), nrm[...], preferred_element_type=jnp.float32
-        ).astype(jnp.bfloat16)
-    for pair in range(owners // 2):
-        e = 2 * pair
-        both = jnp.concatenate(
-            [placed[e] * valued[e : e + 1, :], placed[e + 1] * valued[e + 1 : e + 2, :]], axis=0
-        )
-        weighting[:, 2 * cap * pair : 2 * cap * (pair + 1)] = both.T.astype(jnp.bfloat16)
+        og[e, :, spare:] = jnp.broadcast_to(valued[:cap, e : e + 1], (cap, 128)).astype(jnp.bfloat16)
 
     def slot_rows(s):
         return pl.ds(pl.multiple_of(s * cap, 16), cap)
@@ -304,7 +289,9 @@
     def activate_tile(j):
         for s in range(per_g):
             y_copy(j * per_g + s, 1 - grp).wait_recv()
-        second = jnp.dot(xb[...], wg[1, j], preferred_element_type=jnp.float32)
+        if j == 2:
+            forward(28)
+        second = jnp.dot(xb[:, :depth], wg[1, j], preferred_element_type=jnp.float32)
         mine = first[j]
         gate = jnp.where(x == 0, mine, second)
         up = jnp.where(x == 0, second, mine)
@@ -312,7 +299,7 @@
         a_copy(c, j).start()
 
     for j in range(3):
-        first[j] = jnp.dot(xb[...], wg[0, j], preferred_element_type=jnp.float32)
+        first[j] = jnp.dot(xb[:, :depth], wg[0, j], preferred_element_type=jnp.float32)
         forward(22 + j)
     activate_tile(0)
     forward(25)
@@ -320,21 +307,51 @@
     forward(26)
     forward(27)
     activate_tile(2)
-    forward(28)
+    forward(29)
     for j in range(3):
         a_copy(1 - c, j).wait_recv()
 
     def quarter(h, core):
         return (x if h == 0 else 1 - x) * 2 + core
 
-    def r_copy(h, j, d):
-        other = (slot + d) % 8
+    pair = z + 1 - 2 * (z % 2)
+    far_slot = jnp.where(z < 2, 4, 0)
+    is_end = jnp.logical_or(z == 0, z == owners - 1)
+    far_rows = pl.ds(pl.multiple_of(far_slot * cap, 16), 4 * cap)
+
+    def near_copy(h, j, k):
+        core = 1 - c if k == 0 else k - 1
+        to = z if k == 0 else pair
+        q, place_at = quarter(h, c), 0 if k == 0 else 1
+        return pltpu.make_async_remote_copy(
+            src_ref=res.at[h, j, slot_rows(to * 2 + core)], dst_ref=back.at[q, j, place_at],
+            send_sem=rs.at[h, j, k], recv_sem=rr.at[q, j, place_at],
+            device_id={"exp": to, "wsh": x * 2 + core}, device_id_type=MESH,
+        )
+
+    def far_copy(h, j):
+        return pltpu.make_async_remote_copy(
+            src_ref=res.at[h, j, far_rows], dst_ref=far.at[h, j], send_sem=fs.at[h, j], recv_sem=fr.at[h, j],
+            device_id={"exp": pair}, device_id_type=MESH,
+        )
+
+    def sum_copy(h, j, k):
+        to = far_slot // 2 + k // 2
         q = quarter(h, c)
         return pltpu.make_async_remote_copy(
-            src_ref=res.at[h, j, slot_rows(other)], dst_ref=back.at[q, j, slot_rows(z)],
-            send_sem=rs.at[h, j, d], recv_sem=rr.at[q, j, z],
-            device_id={"exp": other // 2, "wsh": x * 2 + other % 2}, device_id_type=MESH,
-        )
+            src_ref=summed.at[h, j, pl.ds(k * cap, cap)], dst_ref=back.at[q, j, 2],
+            send_sem=ms.at[h, j, k], recv_sem=rr.at[q, j, 2],
+            device_id={"exp": to, "wsh": x * 2 + k % 2}, device_id_type=MESH,
+        )
+
+    def merge(h, j):
+        @pl.when(jnp.logical_not(is_end))
+        def _():
+            far_copy(h, j).wait_recv()
+            own = res[h, j, far_rows, :].astype(jnp.float32)
+            summed[h, j] = (own + far[h, j].astype(jnp.float32)).astype(jnp.bfloat16)
+            for k in range(4):
+                sum_copy(h, j, k).start()
 
     def project(h, j):
         total = jnp.zeros((act.shape[2], TILE), jnp.float32)
@@ -345,38 +362,69 @@
                 total = total + jnp.dot(
                     act[core, k, :, :lanes], wd[h, j, at : at + lanes], preferred_element_type=jnp.float32
                 )
-        res[h, j] = total.astype(jnp.bfloat16)
-        for d in (4, 5, 2, 3, 6, 7, 1):
-            r_copy(h, j, d).start()
-        back[quarter(h, c), j, slot_rows(z), :] = res[h, j, slot_rows(slot), :]
+        weight = xb[:, spare : spare + 1].astype(jnp.float32)
+        res[h, j] = (total.astype(jnp.bfloat16).astype(jnp.float32) * weight).astype(jnp.bfloat16)
+
+        @pl.when(is_end)
+        def _():
+            far_copy(h, j).start()
+
+        for k in (1, 2, 0):
+            near_copy(h, j, k).start()
+        back[quarter(h, c), j, 0] = res[h, j, slot_rows(slot), :]
 
     def combine(h, j):
         for core in range(2):
             q = quarter(h, core)
-            for e in range(4):
-                @pl.when(jnp.logical_or(core != c, e != z))
-                def _():
-                    pltpu.make_async_remote_copy(
-                        src_ref=res.at[h, j, slot_rows(0)], dst_ref=back.at[q, j, slot_rows(e)],
-                        send_sem=rs.at[h, j, 1], recv_sem=rr.at[q, j, e],
-                        device_id={"wsh": mate}, device_id_type=MESH,
-                    ).wait_recv()
-            mixed = jnp.dot(weighting[...], back[q, j], preferred_element_type=jnp.float32)
+
+            def landed(k):
+                pltpu.make_async_remote_copy(
+                    src_ref=res.at[h, j, slot_rows(0)], dst_ref=back.at[q, j, k], send_sem=rs.at[h, j, 0],
+                    recv_sem=rr.at[q, j, k], device_id={"wsh": mate}, device_id_type=MESH,
+                ).wait_recv()
+
+            @pl.when(core != c)
+            def _():
+                landed(0)
+
+            landed(1)
+            landed(2)
+            mixed = back[q, j, 0].astype(jnp.float32) + back[q, j, 1].astype(jnp.float32)
+            mixed = mixed + back[q, j, 2].astype(jnp.float32)
             lanes = min(TILE, width - j * TILE)
             at = pl.multiple_of(q * width + j * TILE, 16)
+            mixed = jnp.concatenate([mixed, jnp.zeros((tokens - cap, TILE), jnp.float32)], axis=0)
             out[pl.ds(at, lanes), :] = mixed.T[:lanes].astype(jnp.bfloat16)
 
+    forward(30)
     for j in range(3):
         project(0, j)
-        forward(29 + j)
-    for j in range(3):
-        for i in range(max(32, count_g + per_d * j), count_g + per_d * (j + 1)):
-            forward(i)
-        for s in range(per_d):
-            y_copy(count_g + j * per_d + s, 1 - grp).wait_recv()
-        project(1, j)
-    for j in range(3):
-        combine(0, j)
+        forward(31 + j)
+    forward(34)
+    merge(0, 0)
+    forward(35)
+    for s in range(per_d):
+        y_copy(count_g + s, 1 - grp).wait_recv()
+    project(1, 0)
+    forward(36)
+    merge(0, 1)
+    for i in range(37, 40):
+        forward(i)
+    merge(0, 2)
+    for s in range(per_d):
+        y_copy(count_g + per_d + s, 1 - grp).wait_recv()
+    forward(40)
+    project(1, 1)
+    forward(41)
+    merge(1, 0)
+    combine(0, 0)
+    for s in range(per_d):
+        y_copy(count_g + 2 * per_d + s, 1 - grp).wait_recv()
+    project(1, 2)
+    merge(1, 1)
+    combine(0, 1)
+    combine(0, 2)
+    merge(1, 2)
     for j in range(3):
         combine(1, j)
 
@@ -391,8 +439,17 @@
         a_copy(c, j).wait_send()
     for h in range(2):
         for j in range(3):
-            for d in range(1, 8):
-                r_copy(h, j, d).wait_send()
+            for k in range(3):
+                near_copy(h, j, k).wait_send()
+
+            @pl.when(is_end)
+            def _():
+                far_copy(h, j).wait_send()
+
+            @pl.when(jnp.logical_not(is_end))
+            def _():
+                for k in range(4):
+                    sum_copy(h, j, k).wait_send()
 
 
 def fused_device(
@@ -410,7 +467,13 @@
     inner = down_codes.shape[1]
     owners = lax.axis_size("exp")
     cap = min(tokens // 2, tokens * expert_ids.shape[1] // owners)
+    if expert_ids.shape[1] != owners:
+        return per_device(
+            hidden_in, norm_gain, expert_ids, gate_weights,
+            gate_up_codes, gate_up_scales, down_codes, down_scales,
+        )
     rows = 2 * owners * cap
+    span = (pl.cdiv(depth, 128) + 1) * 128
     vmem = pl.BlockSpec(memory_space=pltpu.VMEM)
     hbm = pl.BlockSpec(memory_space=pl.ANY)
     bf16, f32 = jnp.bfloat16, jnp.float32
@@ -426,19 +489,20 @@
             pltpu.VMEM((inner, width), bf16),
             pltpu.VMEM((2, tiles, depth, TILE), bf16),
             pltpu.VMEM((2, tiles, inner, TILE), bf16),
-            pltpu.VMEM((tokens, depth), bf16),
-            pltpu.VMEM((tokens, owners * cap), bf16),
-            pltpu.VMEM((owners, cap, depth), bf16),
-            pltpu.VMEM((rows, depth), bf16),
+            pltpu.VMEM((owners, cap, span), bf16),
+            pltpu.VMEM((rows, span), bf16),
             pltpu.VMEM((tiles, rows, TILE), f32),
             pltpu.VMEM((2, tiles, rows, TILE), bf16),
             pltpu.VMEM((2, tiles, rows, TILE), bf16),
-            pltpu.VMEM((4, tiles, owners * cap, TILE), bf16),
+            pltpu.VMEM((2, tiles, rows // 2, TILE), bf16),
+            pltpu.VMEM((2, tiles, rows // 2, TILE), bf16),
+            pltpu.VMEM((4, tiles, 3, cap, TILE), bf16),
             dma((4,)),
             dma((42,)), dma((42,)), dma((42,)), dma((42,)),
             dma((4,)), dma((4,)), dma((4,)), dma((4,)),
             dma((3,)), dma((3,)),
-            dma((2, tiles, 8)), dma((4, tiles, owners)),
+            dma((2, tiles, 3)), dma((4, tiles, 3)),
+            dma((2, tiles)), dma((2, tiles)), dma((2, tiles, 4)),
         ],
         compiler_params=pltpu.CompilerParams(
             collective_id=0, has_side_effects=True, vmem_limit_bytes=58 * 1024 * 1024

time: 107 us -> 103 us (0.963)
  Pallas kernels: 105 us -> 100 us
    pallas_call x1, Pallas kernels: 105 us -> 100 us  [fused_device(): pl.pallas_call(fused_kernel, out_shape=jax.ShapeDtypeStruct((depth, token...]
where the time goes in v4:
time: 103 us; the launch traced here: 102 us
  Pallas kernels  100 us (97%)
  local copies, waits for them, and re-layouts  2.03 us (2%)
    pallas_call x1, Pallas kernels, fused_device(): pl.pallas_call(fused_kernel, out_shape=jax.ShapeDtypeStruct((depth, token...  100 us

profile of v4, /device:TPU:0, one launch (start us, length us, event | category | flops | bytes accessed | tf_op | source)
XLA Modules:
  0.0 102.4 jit_solution(8937055842325000644)
XLA Ops:
  0.0 100.3 %moe_block.1 = bf16[2880,128]{1,0:T(8,128)(2,1)} custom-call(bf16[2880,128]{1,0:T(8,128)(2,1)} %bitcast.9, f32[2880]{0:T(1024)} %gain.1, s32[4,128]{1,0:T(4,128)} %bitcast.12, bf16[4,128]{1,0:T(4,128)(2,1)} %bitcast.13, bf16[1,720,2880]{2,1,0:T(8,128)(2,1)} %bitcast.7, s32[90,1,720]{2,1,0:T(1,128)} %bitcast.10, bf16[1,1440,720]{2,1,0:T(8,128)(2,1)} %dnc.1, ...), custom_call_target="tpu_custom_call" | custom-call | tf_op jit(solution)/shard_map/moe_block/pallas_call | solution.py:482
  100.3 2.0 %copy.10 = bf16[128,2880]{0,1:T(8,128)(2,1)} copy(bf16[128,2880]{0,1:T(8,128)(2,1)} %bitcast.8) | data formatting | bytes 1474560

commit v5 on v4

--- a/solution.py
+++ b/solution.py
@@ -317,7 +317,6 @@
     pair = z + 1 - 2 * (z % 2)
     far_slot = jnp.where(z < 2, 4, 0)
     is_end = jnp.logical_or(z == 0, z == owners - 1)
-    far_rows = pl.ds(pl.multiple_of(far_slot * cap, 16), 4 * cap)
 
     def near_copy(h, j, k):
         core = 1 - c if k == 0 else k - 1
@@ -329,9 +328,10 @@
             device_id={"exp": to, "wsh": x * 2 + core}, device_id_type=MESH,
         )
 
-    def far_copy(h, j):
-        return pltpu.make_async_remote_copy(
-            src_ref=res.at[h, j, far_rows], dst_ref=far.at[h, j], send_sem=fs.at[h, j], recv_sem=fr.at[h, j],
+    def far_copy(h, j, k):
+        return pltpu.make_async_remote_copy(
+            src_ref=res.at[h, j, slot_rows(far_slot + k)], dst_ref=far.at[h, j, pl.ds(k * cap, cap)],
+            send_sem=fs.at[h, j, k], recv_sem=fr.at[h, j, k],
             device_id={"exp": pair}, device_id_type=MESH,
         )
 
@@ -347,10 +347,11 @@
     def merge(h, j):
         @pl.when(jnp.logical_not(is_end))
         def _():
-            far_copy(h, j).wait_recv()
-            own = res[h, j, far_rows, :].astype(jnp.float32)
-            summed[h, j] = (own + far[h, j].astype(jnp.float32)).astype(jnp.bfloat16)
             for k in range(4):
+                rows = pl.ds(k * cap, cap)
+                far_copy(h, j, k).wait_recv()
+                own = res[h, j, slot_rows(far_slot + k), :].astype(jnp.float32)
+                summed[h, j, rows, :] = (own + far[h, j, rows, :].astype(jnp.float32)).astype(jnp.bfloat16)
                 sum_copy(h, j, k).start()
 
     def project(h, j):
@@ -367,7 +368,8 @@
 
         @pl.when(is_end)
         def _():
-            far_copy(h, j).start()
+            for k in range(4):
+                far_copy(h, j, k).start()
 
         for k in (1, 2, 0):
             near_copy(h, j, k).start()
@@ -444,7 +446,8 @@
 
             @pl.when(is_end)
             def _():
-                far_copy(h, j).wait_send()
+                for k in range(4):
+                    far_copy(h, j, k).wait_send()
 
             @pl.when(jnp.logical_not(is_end))
             def _():
@@ -502,7 +505,7 @@
             dma((4,)), dma((4,)), dma((4,)), dma((4,)),
             dma((3,)), dma((3,)),
             dma((2, tiles, 3)), dma((4, tiles, 3)),
-            dma((2, tiles)), dma((2, tiles)), dma((2, tiles, 4)),
+            dma((2, tiles, 4)), dma((2, tiles, 4)), dma((2, tiles, 4)),
         ],
         compiler_params=pltpu.CompilerParams(
             collective_id=0, has_side_effects=True, vmem_limit_bytes=58 * 1024 * 1024

time: 103 us -> 101 us (0.981)
  Pallas kernels: 100 us -> 98.6 us
    pallas_call x1, Pallas kernels: 100 us -> 98.6 us  [fused_device(): pl.pallas_call(fused_kernel, out_shape=jax.ShapeDtypeStruct((depth, token...]
where the time goes in v5:
time: 101 us
  Pallas kernels  98.6 us (98%)
  local copies, waits for them, and re-layouts  2.03 us (2%)
    pallas_call x1, Pallas kernels, fused_device(): pl.pallas_call(fused_kernel, out_shape=jax.ShapeDtypeStruct((depth, token...  98.6 us
    unnamed x1, local copies, waits for them, and re-layouts  2.03 us

profile of v5, /device:TPU:0, one launch (start us, length us, event | category | flops | bytes accessed | tf_op | source)
XLA Modules:
  0.0 100.7 jit_solution(5644522219537725949)
XLA Ops:
  0.0 98.6 %moe_block.1 = bf16[2880,128]{1,0:T(8,128)(2,1)} custom-call(bf16[2880,128]{1,0:T(8,128)(2,1)} %bitcast.9, f32[2880]{0:T(1024)} %gain.1, s32[4,128]{1,0:T(4,128)} %bitcast.12, bf16[4,128]{1,0:T(4,128)(2,1)} %bitcast.13, bf16[1,720,2880]{2,1,0:T(8,128)(2,1)} %bitcast.7, s32[90,1,720]{2,1,0:T(1,128)} %bitcast.10, bf16[1,1440,720]{2,1,0:T(8,128)(2,1)} %dnc.1, ...), custom_call_target="tpu_custom_call" | custom-call | tf_op jit(solution)/shard_map/moe_block/pallas_call | solution.py:485
  98.7 2.0 %copy.10 = bf16[128,2880]{0,1:T(8,128)(2,1)} copy(bf16[128,2880]{0,1:T(8,128)(2,1)} %bitcast.8) | data formatting | bytes 1474560
